TPU v7x, 32 devices: a whole 2x2x4 slice. The times are simulated.
32 devices in a mesh: ctx: 2 (over x), row: 2 (over core), exp: 8 (over z, y).
Axes of the slice: x: 2, y: 2, z: 4, core: 2. Of those that a mesh axis runs over, the one named last changes fastest.
Arguments:
- queries: bfloat16 [64, 128, 576], P(('row', 'exp')), may hold values from -10 to 10
- latent_cache: bfloat16 [64, 8192, 576], P(('row', 'exp'), 'ctx'), may hold values from -6 to 6
- lengths: int32 [64], P(('row', 'exp')), may hold values from 512 to 8192, as said below
- w_value: bfloat16 [128, 512, 128], P(('ctx', 'exp')), may hold values from -0.25 to 0.25
- w_out: bfloat16 [16384, 7168], P(('ctx', 'exp')), may hold values from -0.0625 to 0.0625
- stream: bfloat16 [64, 7168], P(('row', 'exp'), 'ctx'), may hold values from -6 to 6
- norm_gain: float32 [7168], P('ctx'), may hold values from 0.1 to 1.9
- expert_ids: int32 [64, 8], P(('row', 'exp')), may hold values from 0 to 15, all different within a row; in each aligned block of 4 rows (0 to 3, 4 to 7, ...) at most 2 rows name the same one
- gate_weights: float32 [64, 8], P(('row', 'exp')), may hold values from 0.1 to 0.6
- w_gate: bfloat16 [16, 7168, 1024], P(('row', 'exp'), 'ctx'), may hold values from -0.0625 to 0.0625
- w_up: bfloat16 [16, 7168, 1024], P(('row', 'exp'), 'ctx'), may hold values from -0.0625 to 0.0625
- w_down: bfloat16 [16, 1024, 7168], P(('row', 'exp'), None, 'ctx'), may hold values from -0.1875 to 0.1875
Outputs:
- layer_out: bfloat16 [64, 7168], P(('row', 'exp'), 'ctx')
Inputs may be any that keep to these rules, and one draw needn't show every extreme that they name: `lengths`: some row has 8192 live positions and some row 512. `expert_ids`: each row names 8 different experts; among the 4 rows of one device no expert is named by more than 2 rows.
All inputs are finite; a program needn't handle non-finite values.
Results may differ from a plain program's by a relative error of at most 0.012.
Values may be sent and summed in bfloat16 or wider, within the bound.
A program may use at most 128 MiB of HBM per device.

v0:
```python
import jax
import jax.numpy as jnp
from jax import lax
from jax.sharding import PartitionSpec as P

D = 7168
QK_HEAD = 192


epsilon = 1e-06


def merge_blocks(outputs, maxima, totals):
    top_value = jnp.max(maxima, axis=0)
    factor = jnp.exp(maxima - top_value[None])
    numer = jnp.sum(factor[..., None] * outputs, axis=0)
    denom = jnp.sum(factor * totals, axis=0)
    return (numer / denom[..., None]).astype(jnp.bfloat16)


def on_device(
    queries,
    latent_cache,
    lengths,
    w_value,
    w_out,
    stream,
    norm_gain,
    expert_ids,
    gate_weights,
    w_gate,
    w_up,
    w_down,
):
    n_ctx = lax.axis_size("ctx")
    n_row = lax.axis_size("row")
    n_exp = lax.axis_size("exp")
    groups = queries.shape[0]
    block = latent_cache.shape[1]
    per_dev = w_value.shape[0]
    latent = w_value.shape[1]
    scores = jnp.einsum(
        "bhw,btw->bht", queries, latent_cache, preferred_element_type=jnp.float32
    ) * QK_HEAD ** (-0.5)
    position = lax.axis_index("ctx") * block + jnp.arange(block, dtype=jnp.int32)
    live = (position[None, :] < lengths[:, None])[:, None, :]
    block_max = jnp.max(jnp.where(live, scores, -jnp.inf), axis=2)
    shift_by = jnp.where(jnp.isfinite(block_max), block_max, 0.0)
    weights = jnp.where(live, jnp.exp(scores - shift_by[..., None]), 0.0)
    totals = jnp.sum(weights, axis=2)
    latent_out = jnp.einsum(
        "bht,btl->bhl",
        weights.astype(jnp.bfloat16),
        latent_cache[:, :, :latent],
        preferred_element_type=jnp.float32,
    )
    outputs, maxima, sums = (
        lax.all_to_all(
            latent_out.reshape(1, groups, n_ctx * n_exp, per_dev, latent),
            ("ctx", "exp"),
            split_axis=2,
            concat_axis=0,
            tiled=True,
        ),
        lax.all_to_all(
            block_max.reshape(1, groups, n_ctx * n_exp, per_dev),
            ("ctx", "exp"),
            split_axis=2,
            concat_axis=0,
            tiled=True,
        ),
        lax.all_to_all(
            totals.reshape(1, groups, n_ctx * n_exp, per_dev),
            ("ctx", "exp"),
            split_axis=2,
            concat_axis=0,
            tiled=True,
        ),
    )
    gathered_rows = n_exp * groups
    attended = merge_blocks(
        outputs.reshape(n_ctx, gathered_rows, per_dev, latent),
        maxima.reshape(n_ctx, gathered_rows, per_dev),
        sums.reshape(n_ctx, gathered_rows, per_dev),
    )
    values = jnp.einsum("nhl,hlv->nhv", attended, w_value, preferred_element_type=jnp.float32)
    values = values.astype(jnp.bfloat16).reshape(gathered_rows, -1)
    split_out = w_out.reshape(w_out.shape[0], n_ctx, -1)
    term_rows = jnp.einsum(
        "nk,kcd->cnd", values, split_out, preferred_element_type=jnp.float32
    ).reshape(n_ctx * gathered_rows, -1)
    attn_out = lax.psum_scatter(term_rows, ("ctx", "exp"), scatter_dimension=0, tiled=True)
    hidden = lax.optimization_barrier((stream.astype(jnp.float32) + attn_out).astype(jnp.bfloat16))
    experts = n_row * n_exp
    picks = expert_ids.shape[1]
    capacity = max(2, (groups * picks + experts - 1) // experts)
    expert_range = jnp.arange(experts, dtype=jnp.int32)
    onehot = expert_ids[:, :, None] == expert_range[None, None, :]
    named = jnp.sum(onehot.astype(jnp.int32), axis=1)
    slot_of = jnp.cumsum(named, axis=0) - named
    slot_match = slot_of[:, :, None] == jnp.arange(capacity, dtype=jnp.int32)[None, None, :]
    placed = (named[:, :, None] == 1) & slot_match
    outgoing = jnp.einsum(
        "bxs,bd->xsd", placed.astype(jnp.bfloat16), hidden, preferred_element_type=jnp.float32
    ).astype(jnp.bfloat16)
    width_dev = outgoing.shape[2]
    arrived = lax.all_to_all(outgoing, ("row", "exp"), split_axis=0, concat_axis=0, tiled=True)
    arrived = arrived.reshape(experts * capacity, width_dev)
    arrived_wide = arrived.astype(jnp.float32)
    sumsq = jnp.sum(arrived_wide * arrived_wide, axis=1)
    scaled = (arrived_wide * norm_gain[None, :]).astype(jnp.bfloat16)
    gate_part = jnp.dot(scaled, w_gate[0], preferred_element_type=jnp.float32)
    up_part = jnp.dot(scaled, w_up[0], preferred_element_type=jnp.float32)
    gate_part, up_part, sumsq = lax.psum((gate_part, up_part, sumsq), "ctx")
    inverse = lax.rsqrt(sumsq / D + epsilon)[:, None]
    active = (jax.nn.silu(inverse * gate_part) * (inverse * up_part)).astype(jnp.bfloat16)
    produced = jnp.dot(active, w_down[0], preferred_element_type=jnp.float32).astype(jnp.bfloat16)
    returned = lax.all_to_all(
        produced.reshape(experts, capacity, width_dev),
        ("row", "exp"),
        split_axis=0,
        concat_axis=0,
        tiled=True,
    )
    weighted = jnp.sum(gate_weights[:, :, None] * onehot.astype(jnp.float32), axis=1)
    combine = weighted[:, :, None] * slot_match.astype(jnp.float32)
    mixture = jnp.einsum(
        "bxs,xsd->bd", combine, returned.astype(jnp.float32), precision=lax.Precision.HIGHEST
    )
    return (hidden.astype(jnp.float32) + mixture).astype(jnp.bfloat16)


def solution(mesh):
    placed = (
        P(("row", "exp"), None, None),
        P(("row", "exp"), "ctx", None),
        P(("row", "exp")),
        P(("ctx", "exp"), None, None),
        P(("ctx", "exp"), None),
        P(("row", "exp"), "ctx"),
        P("ctx"),
        P(("row", "exp"), None),
        P(("row", "exp"), None),
        P(("row", "exp"), "ctx", None),
        P(("row", "exp"), "ctx", None),
        P(("row", "exp"), None, "ctx"),
    )
    return jax.shard_map(
        on_device, mesh=mesh, in_specs=placed, out_specs=P(("row", "exp"), "ctx"), check_vma=False
    )
```

profile of v0, /device:TPU:0, one launch (start us, length us, event | category | flops | bytes accessed | tf_op | source)
XLA Modules:
  0.0 277.6 jit_solution(3147298467909820867)
XLA Ops:
  6.5 0.0 copy-start
  6.5 0.8 broadcast_compare_fusion
  7.4 8.9 %select_reduce_fusion = (f32[4,128]{1,0:T(4,128)S(1)}, f32[4,128,4096]{2,1,0:T(8,128)S(1)}) fusion(pred[4,4096]{1,0:T(4,128)(4,1)S(1)} %broadcast_compare_fusion, bf16[4,128,576]{1,2,0:T(8,128)(2,1)} %param.12, bf16[4,4096,576]{1,2,0:T(8,128)(2,1)} %param.13), kind=kOutput, calls=%fused_computation.6 | convolution fusion | flops 2422210048 | bytes 27871232 | tf_op jit(solution)/shard_map/bhw,btw->bht/dot_general | solution.py:42
  16.3 0.0 copy-start.1
  16.3 3.2 %copy-done.1 = f32[4,128,4096]{2,1,0:T(8,128)} copy-done((f32[4,128,4096]{2,1,0:T(8,128)}, f32[4,128,4096]{2,1,0:T(8,128)S(1)}, u32[]{:S(2)}) %copy-start.1) | copy-done | bytes 8388632
  19.5 2.2 fusion.11
  21.7 0.1 reshape.115
  21.8 0.6 copy.49
  22.4 8.3 %all-to-all-start.2 = ((f32[1,4,16,8]{3,1,0,2:T(4,128)}), f32[1,4,16,8]{3,1,0,2:T(4,128)S(1)}, u32[]{:S(2)}, u32[]{:S(2)}) async-start(f32[1,4,16,8]{3,1,0,2:T(4,128)} %copy.49), calls=%async_computation.2 | async-start | bytes 65536 | tf_op jit(solution)/shard_map/all_to_all | solution.py:72
  30.8 0.1 reshape.111
  30.8 0.6 copy.46
  31.5 6.7 %all-to-all-done.2 = f32[1,4,16,8]{3,1,0,2:T(4,128)S(1)} async-done(((f32[1,4,16,8]{3,1,0,2:T(4,128)}), f32[1,4,16,8]{3,1,0,2:T(4,128)S(1)}, u32[]{:S(2)}, u32[]{:S(2)}) %all-to-all-start.2) | async-done | bytes 2080 | tf_op jit(solution)/shard_map/all_to_all | solution.py:72
  38.2 3.5 %all-to-all-start = ((f32[1,4,16,8]{3,1,0,2:T(4,128)}), f32[1,4,16,8]{3,1,0,2:T(4,128)S(1)}, u32[]{:S(2)}, u32[]{:S(2)}) async-start(f32[1,4,16,8]{3,1,0,2:T(4,128)} %copy.46), calls=%async_computation | async-start | bytes 65536 | tf_op jit(solution)/shard_map/all_to_all | solution.py:65
  41.6 11.2 %fusion.23 = f32[1,4,16,8,512]{4,3,2,1,0:T(8,128)S(1)} fusion(bf16[4,4096,576]{1,2,0:T(8,128)(2,1)} %param.13, f32[4,128,4096]{2,1,0:T(8,128)} %copy-done.1, f32[4,128]{1,0:T(4,128)S(1)} %is-finite_select_fusion, pred[4,4096]{1,0:T(4,128)(4,1)S(1)} %broadcast_compare_fusion), kind=kOutput, calls=%fused_computation.24 | convolution fusion | flops 2155872256 | bytes 26232832 | tf_op jit(solution)/shard_map/bht,btl->bhl/dot_general | solution.py:51
  52.9 1.1 copy.48
  53.9 0.0 all-to-all-done
  53.9 6.9 %all-to-all-start.1 = ((f32[1,4,16,8,512]{4,3,1,0,2:T(8,128)}), f32[1,4,16,8,512]{4,3,1,0,2:T(8,128)S(1)}, u32[]{:S(2)}, u32[]{:S(2)}) async-start(f32[1,4,16,8,512]{4,3,1,0,2:T(8,128)} %copy.48), calls=%async_computation.1 | async-start | bytes 2097152 | tf_op jit(solution)/shard_map/all_to_all | solution.py:58
  60.8 0.0 all-reduce.5.cloned.1.call-start
  60.9 24.3 %all-to-all-done.1 = f32[1,4,16,8,512]{4,3,1,0,2:T(8,128)S(1)} async-done(((f32[1,4,16,8,512]{4,3,1,0,2:T(8,128)}), f32[1,4,16,8,512]{4,3,1,0,2:T(8,128)S(1)}, u32[]{:S(2)}, u32[]{:S(2)}) %all-to-all-start.1) | async-done | bytes 1048608 | tf_op jit(solution)/shard_map/all_to_all | solution.py:58
  85.2 0.1 multiply_reduce_fusion
  85.3 0.1 divide_convert_fusion
  85.5 0.0 copy-done
  85.5 0.3 fusion.28
  85.9 0.0 copy-start.4
  85.9 0.0 copy-start.6
  85.9 0.0 copy-start.2
  85.9 0.0 copy-start.3
  85.9 7.5 %fusion.2 = f32[32,2,3584]{2,0,1:T(8,128)} fusion(bf16[32,1024,1]{1,0,2:T(8,128)(2,1)S(1)} %reshape.121, bf16[128,2,8,3584]{3,2,1,0:T(8,128)(2,1)} %bitcast.53), kind=kOutput, calls=%fused_computation.2 | convolution fusion | flops 469762048 | bytes 15663104 | tf_op jit(solution)/shard_map/nk,kcd->cnd/dot_general | solution.py:89
  93.5 0.0 all-reduce.5.cloned.1.call-update
  93.5 0.0 all-reduce.7.cloned.1.call-start
  93.5 0.0 copy-done.4
  93.5 0.1 convert_reduce_fusion
  93.7 0.0 copy-done.6
  93.7 0.6 dynamic-slice
  94.9 107.5 %all-reduce.5.cloned.1.call-done = f32[64,3584]{1,0:T(8,128)} async-done(((f32[64,3584]{1,0:T(8,128)}), f32[64,3584]{1,0:T(8,128)}) %all-reduce.5.cloned.1.call-update) | async-done | bytes 917520
  202.5 0.0 copy-done.2
  202.5 0.9 fusion.35
  203.4 0.3 convolution_convert_fusion
  203.7 0.2 copy.53
  203.9 13.8 %all_to_all.55 = bf16[16,2,3584]{2,1,0:T(2,128)(2,1)S(1)} all-to-all(bf16[16,2,3584]{2,1,0:T(2,128)(2,1)S(1)} %copy.53), channel_id=1, replica_groups=mesh['ctx'=2,'row'=2,'exp'=8] {'row','exp'}, dimensions={0} | all-to-all | bytes 458752 | tf_op jit(solution)/shard_map/all_to_all | solution.py:107
  217.7 0.0 copy-done.3
  217.7 0.1 fusion.29
  217.9 0.3 copy.56
  218.1 0.1 convert_element_type.64
  218.2 5.1 %fusion.7 = f32[32,1024]{1,0:T(8,128)} fusion(bf16[32,3584]{1,0:T(8,128)(2,1)S(1)} %convert_element_type.64, bf16[1,3584,1024]{2,1,0:T(8,128)(2,1)} %param.22), kind=kOutput, calls=%fused_computation.9 | convolution fusion | flops 234881024 | bytes 7700480 | tf_op jit(solution)/shard_map/dot_general | solution.py:113
  223.3 0.0 copy-start.5
  223.3 5.1 %fusion.9 = f32[32,1024]{1,0:T(8,128)} fusion(bf16[32,3584]{1,0:T(8,128)(2,1)S(1)} %convert_element_type.64, bf16[1,3584,1024]{2,1,0:T(8,128)(2,1)} %param.21), kind=kOutput, calls=%fused_computation.11 | convolution fusion | flops 234881024 | bytes 7700480 | tf_op jit(solution)/shard_map/dot_general | solution.py:112
  228.4 0.0 all-reduce.7.cloned.1.call-update
  228.5 0.1 copy.55
  228.6 0.1 reduce_sum.62
  228.6 5.0 %psum.21 = f32[32]{0:T(128)S(1)} all-reduce(f32[32]{0:T(128)S(1)} %reduce_sum.62), channel_id=1, replica_groups=mesh['ctx'=2,'row'=2,'exp'=8] {'ctx'}, use_global_device_ids=true, to_apply=%region_10.11 | all-reduce | flops 32 | bytes 256 | tf_op jit(solution)/shard_map/psum | solution.py:114
  233.6 15.5 %all-reduce.7.cloned.1.call-done = (f32[32,1024]{1,0:T(8,128)}, f32[32,1024]{1,0:T(8,128)}) async-done(((f32[32,1024]{1,0:T(8,128)}, f32[32,1024]{1,0:T(8,128)}), (f32[32,1024]{1,0:T(8,128)}, f32[32,1024]{1,0:T(8,128)})) %all-reduce.7.cloned.1.call-update) | async-done | bytes 262160 | tf_op jit(solution)/shard_map/psum | solution.py:114
  249.1 4.6 %fusion.13 = bf16[32,3584]{1,0:T(8,128)(2,1)S(1)} fusion(bf16[1,1024,3584]{2,1,0:T(8,128)(2,1)} %param.23, f32[32,1024]{1,0:T(8,128)} %get-tuple-element.5, f32[32,1024]{1,0:T(8,128)} %get-tuple-element.6, f32[32]{0:T(128)S(1)} %add_rsqrt_fusion), kind=kOutput, calls=%fused_computation.15 | convolution fusion | flops 235257856 | bytes 7831680 | tf_op jit(solution)/shard_map/dot_general | solution.py:117
  253.7 0.8 reshape.120
  254.5 5.6 %all-to-all-start.4 = ((bf16[16,2,3584]{2,1,0:T(2,128)(2,1)}), bf16[16,2,3584]{2,1,0:T(2,128)(2,1)S(1)}, u32[]{:S(2)}, u32[]{:S(2)}) async-start(bf16[16,2,3584]{2,1,0:T(2,128)(2,1)} %reshape.120), calls=%async_computation.4 | async-start | bytes 458752 | tf_op jit(solution)/shard_map/all_to_all | solution.py:118
  260.1 0.0 copy-done.5
  260.1 0.1 select_reduce_fusion.1
  260.2 9.6 %all-to-all-done.4 = bf16[16,2,3584]{2,1,0:T(2,128)(2,1)S(1)} async-done(((bf16[16,2,3584]{2,1,0:T(2,128)(2,1)}), bf16[16,2,3584]{2,1,0:T(2,128)(2,1)S(1)}, u32[]{:S(2)}, u32[]{:S(2)}) %all-to-all-start.4) | async-done | bytes 229408 | tf_op jit(solution)/shard_map/all_to_all | solution.py:118
  269.8 0.9 fusion.17
  (10 shorter events, 0.2 us)
Async XLA Ops:
  6.5 78.9 %copy-start = (bf16[8,512,128]{2,1,0:T(8,128)(2,1)S(1)}, bf16[8,512,128]{2,1,0:T(8,128)(2,1)}, u32[]{:S(2)}) copy-start(bf16[8,512,128]{2,1,0:T(8,128)(2,1)} %param.15) | copy-start | bytes 3145732
  16.3 3.2 %copy-start.1 = (f32[4,128,4096]{2,1,0:T(8,128)}, f32[4,128,4096]{2,1,0:T(8,128)S(1)}, u32[]{:S(2)}) copy-start(f32[4,128,4096]{2,1,0:T(8,128)S(1)} %get-tuple-element.12) | copy-start | bytes 25165828
  22.4 15.7 %all-to-all-start.2 = ((f32[1,4,16,8]{3,1,0,2:T(4,128)}), f32[1,4,16,8]{3,1,0,2:T(4,128)S(1)}, u32[]{:S(2)}, u32[]{:S(2)}) async-start(f32[1,4,16,8]{3,1,0,2:T(4,128)} %copy.49), calls=%async_computation.2 | async-start | bytes 65536 | tf_op jit(solution)/shard_map/all_to_all | solution.py:72
  38.2 15.8 %all-to-all-start = ((f32[1,4,16,8]{3,1,0,2:T(4,128)}), f32[1,4,16,8]{3,1,0,2:T(4,128)S(1)}, u32[]{:S(2)}, u32[]{:S(2)}) async-start(f32[1,4,16,8]{3,1,0,2:T(4,128)} %copy.46), calls=%async_computation | async-start | bytes 65536 | tf_op jit(solution)/shard_map/all_to_all | solution.py:65
  53.9 31.3 %all-to-all-start.1 = ((f32[1,4,16,8,512]{4,3,1,0,2:T(8,128)}), f32[1,4,16,8,512]{4,3,1,0,2:T(8,128)S(1)}, u32[]{:S(2)}, u32[]{:S(2)}) async-start(f32[1,4,16,8,512]{4,3,1,0,2:T(8,128)} %copy.48), calls=%async_computation.1 | async-start | bytes 2097152 | tf_op jit(solution)/shard_map/all_to_all | solution.py:58
  60.8 141.6 %all-reduce.5.cloned.1.call-start = ((), (), s32[]{:S(2)}) async-start(), calls=%async_computation.5 | async-start | bytes 1835008
  85.9 7.7 %copy-start.4 = (s32[4,8]{1,0:T(4,128)S(1)}, s32[4,8]{1,0:T(4,128)}, u32[]{:S(2)}) copy-start(s32[4,8]{1,0:T(4,128)} %param.19) | copy-start | bytes 388
  85.9 7.8 %copy-start.6 = (u32[32]{0:T(128)S(1)}, u32[32]{0:T(128)}, u32[]{:S(2)}) copy-start(u32[32]{0:T(128)} %constant.43) | copy-start | bytes 388
  85.9 116.6 %copy-start.2 = (bf16[4,3584]{1,0:T(4,128)(2,1)S(1)}, bf16[4,3584]{1,0:T(4,128)(2,1)}, u32[]{:S(2)}) copy-start(bf16[4,3584]{1,0:T(4,128)(2,1)} %param.17) | copy-start | bytes 86020
  85.9 131.8 %copy-start.3 = (f32[3584]{0:T(1024)S(1)}, f32[3584]{0:T(1024)}, u32[]{:S(2)}) copy-start(f32[3584]{0:T(1024)} %param.18) | copy-start | bytes 43012
  93.5 155.6 %all-reduce.7.cloned.1.call-start = ((), (), s32[]{:S(2)}) async-start(), calls=%async_computation.6 | async-start | bytes 524288 | tf_op jit(solution)/shard_map/psum | solution.py:114
  223.3 36.8 %copy-start.5 = (f32[4,8]{1,0:T(4,128)S(1)}, f32[4,8]{1,0:T(4,128)}, u32[]{:S(2)}) copy-start(f32[4,8]{1,0:T(4,128)} %param.20) | copy-start | bytes 388
  254.5 15.3 %all-to-all-start.4 = ((bf16[16,2,3584]{2,1,0:T(2,128)(2,1)}), bf16[16,2,3584]{2,1,0:T(2,128)(2,1)S(1)}, u32[]{:S(2)}, u32[]{:S(2)}) async-start(bf16[16,2,3584]{2,1,0:T(2,128)(2,1)} %reshape.120), calls=%async_computation.4 | async-start | bytes 458752 | tf_op jit(solution)/shard_map/all_to_all | solution.py:118
Sparse Core Ops, SparseCore 0:
  93.6 108.8 all-reduce.4
  228.6 20.4 all-reduce.6
where the time goes:
time: 278 us
  waiting for transfers between devices  164 us (59%)
  matrix products  44 us (16%)
  starting transfers between devices  24.4 us (9%)
  blocking collectives  18.8 us (7%)
  between operations  14.3 us (5%)
  local copies, waits for them, and re-layouts  7.9 us (3%)
  other arithmetic  4.6 us (2%)
    unnamed x3, waiting for transfers between devices  108 us
    all_to_all x1, waiting for transfers between devices, on_device(): lax.all_to_all(latent_out.reshape(1, groups, n_ctx * n_exp, per_dev, late...  24.3 us
    psum x1, waiting for transfers between devices, on_device(): gate_part, up_part, sumsq = lax.psum((gate_part, up_part, sumsq), 'ctx')  15.5 us
    all_to_all x1, blocking collectives, on_device(): lax.all_to_all(outgoing, ('row', 'exp'), split_axis=0, concat_axis=0, til...  13.8 us
    dot_general x1, matrix products, on_device(): jnp.einsum('bht,btl->bhl', weights.astype(jnp.bfloat16), latent_cache[:,...  11.2 us
    all_to_all x1, waiting for transfers between devices, on_device(): lax.all_to_all(produced.reshape(experts, capacity, width_dev), ('row', 'e...  9.58 us
    dot_general x1, matrix products, on_device(): jnp.einsum('bhw,btw->bht', queries, latent_cache, preferred_element_type=...  8.88 us
    all_to_all x1, starting transfers between devices, on_device(): lax.all_to_all(totals.reshape(1, groups, n_ctx * n_exp, per_dev), ('ctx',...  8.31 us
  transfers between devices with their start and end apart: 6, of which 5 were waited for; matrix products, arithmetic and copies ran while one was open for 5% of the time, Pallas kernels for 0%

commit v1 on v0

--- a/solution.py
+++ b/solution.py
@@ -1,6 +1,10 @@
+import math
+
 import jax
 import jax.numpy as jnp
 from jax import lax
+from jax.experimental import pallas as pl
+from jax.experimental.pallas import tpu as pltpu
 from jax.sharding import PartitionSpec as P
 
 D = 7168
@@ -130,6 +134,465 @@
     return (hidden.astype(jnp.float32) + mixture).astype(jnp.bfloat16)
 
 
+F32 = jnp.float32
+BF16 = jnp.bfloat16
+MESH = pl.DeviceIdType.MESH
+DEAD = -1e30
+FLOOR = -1e29
+RATE = QK_HEAD ** (-0.5) * math.log2(math.e)
+
+
+def iota(shape, dim):
+    return lax.broadcasted_iota(jnp.int32, shape, dim)
+
+
+def mm(a, b):
+    return jnp.dot(a, b, preferred_element_type=F32)
+
+
+def onehot(cond):
+    return jnp.where(cond, 1.0, 0.0).astype(BF16)
+
+
+def routing(expert, ids, gates, rows, picks):
+    weights, slots = [], []
+    before = jnp.zeros(expert.shape, jnp.int32)
+    for b in range(rows):
+        weight = jnp.zeros(expert.shape, F32)
+        for k in range(picks):
+            weight = jnp.where(expert == ids[b, k], gates[b, k], weight)
+        weights.append(weight)
+        slots.append(before)
+        before = before + jnp.where(weight > 0.0, 1, 0)
+    return weights, slots
+
+
+def layer_kernel(
+    queries, cache_hbm, lengths, wv_hbm, wo_hbm, stream, gain, ids, gates, wg_hbm, wu_hbm, wd_hbm,
+    out,
+    cache, wv, wo, wg, wu, wd,
+    scores, msg, xr, atf, ats, ar, vals, osend, oown, orecv, packed, rsend, rrecv, hid4, blocks,
+    tsend, trecv, xsel, gusend, gurecv, sqsend, sqrecv, made, psend, precv, combine,
+    cache_sem, w_sem, x_ss, x_rs, a_ss, a_rs, o_ss, o_rs, r_ss, r_rs, g_ss, g_rs, t_ss, t_rs,
+    u_ss, u_rs, p_ss, p_rs,
+):
+    rows, heads, _ = queries.shape
+    block = cache_hbm.shape[1]
+    latent = wv_hbm.shape[1]
+    n_exp = lax.axis_size("exp")
+    devs = lax.axis_size("row") * n_exp
+    picks = ids.shape[1]
+    per_dev = wv_hbm.shape[0]
+    width = stream.shape[1]
+    part = width // 4
+    c, r, e = lax.axis_index("ctx"), lax.axis_index("row"), lax.axis_index("exp")
+    g = r * n_exp + e
+    z, y = e // 2, lax.rem(e, 2)
+    half_heads = heads // 2
+
+    def remote(src, dst, ss, rs, ctx=None, row=None, exp=None):
+        where = {
+            "ctx": c if ctx is None else ctx,
+            "row": r if row is None else row,
+            "exp": e if exp is None else exp,
+        }
+        return pltpu.make_async_remote_copy(
+            src_ref=src, dst_ref=dst, send_sem=ss, recv_sem=rs, device_id=where, device_id_type=MESH
+        )
+
+    def each(low, high, body):
+        def step(i, carry):
+            body(i)
+            return carry
+
+        lax.fori_loop(low, high, step, 0)
+
+    def cache_copy(b):
+        slot = lax.rem(b, 2)
+        return pltpu.make_async_copy(cache_hbm.at[b], cache.at[slot], cache_sem.at[slot])
+
+    def half_of(i):
+        side = (1 - c) if i == 0 else c
+        return wo_hbm.at[:, pl.ds(pl.multiple_of(side * width, 128), width)]
+
+    weight_copies = [
+        pltpu.make_async_copy(wv_hbm, wv, w_sem.at[0]),
+        pltpu.make_async_copy(half_of(0), wo.at[0], w_sem.at[1]),
+        pltpu.make_async_copy(half_of(1), wo.at[1], w_sem.at[2]),
+        pltpu.make_async_copy(wg_hbm.at[0], wg, w_sem.at[3]),
+        pltpu.make_async_copy(wu_hbm.at[0], wu, w_sem.at[4]),
+        pltpu.make_async_copy(wd_hbm.at[0], wd, w_sem.at[5]),
+    ]
+
+    cache_copy(0).start()
+    cache_copy(1).start()
+
+    barrier = pltpu.get_barrier_semaphore()
+    pl.semaphore_signal(
+        barrier, inc=1, device_id={"ctx": 1 - c, "row": r, "exp": e}, device_id_type=MESH
+    )
+
+    def greet(d):
+        to = lax.rem(g + d, devs)
+        pl.semaphore_signal(
+            barrier, inc=1, device_id={"ctx": c, "row": to // n_exp, "exp": lax.rem(to, n_exp)},
+            device_id_type=MESH,
+        )
+
+    each(1, devs, greet)
+
+    shape = (devs, 8, 128)
+    expert, sub, lane = iota(shape, 0), iota(shape, 1), iota(shape, 2)
+    weights, slots = routing(expert, ids, gates, rows, picks)
+    tile = jnp.zeros(shape, F32)
+    for b in range(rows):
+        here = ((lane & 3) == b) & (sub == 2 * lax.rem(g, 4) + slots[b])
+        tile = jnp.where(here, weights[b], tile)
+    tsend[...] = tile
+    trecv[g] = tsend[g]
+
+    shape = (32, devs * 16)
+    line, col = iota(shape, 0), iota(shape, 1)
+    weights, slots = routing(col >> 4, ids, gates, rows, picks)
+    comb = jnp.zeros(shape, F32)
+    for b in range(rows):
+        here = ((line & 3) == b) & ((line >> 2) == ((col & 15) >> 1)) & ((col & 1) == slots[b])
+        comb = jnp.where(here, weights[b], comb)
+    high = comb.astype(BF16)
+    combine[0:32, :] = high
+    combine[32:64, :] = (comb - high.astype(F32)).astype(BF16)
+
+    pl.semaphore_wait(barrier, devs)
+
+    def tile_copy(d, back=False):
+        to = lax.rem(g + d, devs)
+        return remote(
+            tsend.at[to], trecv.at[to if back else g], t_ss.at[to], t_rs.at[to if back else g],
+            row=to // n_exp, exp=lax.rem(to, n_exp),
+        )
+
+    each(1, devs, lambda d: tile_copy(d).start())
+
+    def swap(b):
+        return remote(msg.at[b, 1 - c], xr.at[b], x_ss.at[b], x_rs.at[b], ctx=1 - c)
+
+    def att_copy(pair, d, back=False):
+        to = lax.rem(e + d, n_exp)
+        return remote(
+            ats.at[pair, to], ar.at[to if back else e, pair],
+            a_ss.at[pair, to], a_rs.at[pair, to if back else e], exp=to,
+        )
+
+    def attend(b):
+        slot = lax.rem(b, 2)
+        cache_copy(b).wait()
+        query = queries[b]
+        live = lengths[b] - c * block
+        step = 1024
+        tops = []
+        for t in range(block // step):
+            span = slice(t * step, (t + 1) * step)
+            s = lax.dot_general(
+                query, cache[slot, span, :], (((1,), (1,)), ((), ())), preferred_element_type=F32
+            )
+            s = jnp.where(iota(s.shape, 1) + t * step < live, s, DEAD)
+            scores[:, span] = s
+            tops.append(jnp.max(s, axis=1, keepdims=True))
+        top = tops[0]
+        for other in tops[1:]:
+            top = jnp.maximum(top, other)
+        top = jnp.maximum(top, FLOOR).astype(BF16).astype(F32)
+        total = jnp.zeros_like(top)
+        acc = jnp.zeros((heads, latent), F32)
+        for t in range(block // step):
+            span = slice(t * step, (t + 1) * step)
+            p = jnp.exp2((scores[:, span] - top) * RATE)
+            total += jnp.sum(p, axis=1, keepdims=True)
+            acc += mm(p.astype(BF16), cache[slot, span, 0:latent])
+        lane = iota((heads, 128), 1)
+        rest = total - total.astype(BF16).astype(F32)
+        aux = jnp.where(lane == 0, top, jnp.where(lane == 1, total, jnp.where(lane == 2, rest, 0.0)))
+        acc, aux = acc.astype(BF16), aux.astype(BF16)
+        for side in range(2):
+            mine = slice(side * half_heads, (side + 1) * half_heads)
+            msg[b, side, :, 0:latent] = acc[mine]
+            msg[b, side, :, latent : latent + 128] = aux[mine]
+        swap(b).start()
+
+    def merge(b, pair, last):
+        swap(b).wait_recv()
+        one, two = msg[b, c].astype(F32), xr[b].astype(F32)
+
+        def aux_of(m):
+            return m[:, latent : latent + 1], m[:, latent + 1 : latent + 2] + m[:, latent + 2 : latent + 3]
+
+        (top1, sum1), (top2, sum2) = aux_of(one), aux_of(two)
+        top = jnp.maximum(top1, top2)
+        f1, f2 = jnp.exp2((top1 - top) * RATE), jnp.exp2((top2 - top) * RATE)
+        inv = 1.0 / (f1 * sum1 + f2 * sum2)
+        att = (f1 * inv) * one[:, 0:latent] + (f2 * inv) * two[:, 0:latent]
+        att = att.reshape(n_exp, per_dev, latent)
+        if not last:
+            atf[...] = att
+        else:
+            ats[pair] = jnp.concatenate([atf[...], att], axis=1).astype(BF16)
+            ar[e, pair] = ats[pair, e]
+            each(1, n_exp, lambda d: att_copy(pair, d).start())
+
+    def row_step(b):
+        attend(b)
+
+        @pl.when(b < rows - 2)
+        def _():
+            cache_copy(b + 2).start()
+
+        @pl.when(b == 1)
+        def _():
+            merge(0, 0, False)
+            for w in weight_copies[0:3]:
+                w.start()
+
+        @pl.when(b == 2)
+        def _():
+            merge(1, 0, True)
+            for w in weight_copies[3:5]:
+                w.start()
+
+        @pl.when(b == 3)
+        def _():
+            merge(2, 1, False)
+            weight_copies[5].start()
+
+    each(0, rows, row_step)
+    merge(3, 1, True)
+
+    weight_copies[0].wait()
+    for pair in range(2):
+        each(1, n_exp, lambda d: att_copy(pair, d, True).wait_recv())
+    n_rows = n_exp * rows
+    x = ar[...].reshape(n_rows * per_dev, latent)
+    for h in range(per_dev):
+        v = mm(x, wv[h])
+        v = jnp.where((iota(v.shape, 0) & (per_dev - 1)) == h, v, 0.0)
+        v = jnp.sum(v.reshape(n_rows, per_dev, v.shape[1]), axis=1)
+        vals[:, h * v.shape[1] : (h + 1) * v.shape[1]] = v.astype(BF16)
+
+    def term_copy(k):
+        return remote(osend.at[k], orecv.at[k], o_ss.at[k], o_rs.at[k], ctx=1 - c)
+
+    weight_copies[1].wait()
+    for k in range(4):
+        osend[k] = mm(vals[...], wo[0, :, k * part : (k + 1) * part]).astype(BF16)
+        term_copy(k).start()
+    weight_copies[2].wait()
+    for k in range(4):
+        oown[k] = mm(vals[...], wo[1, :, k * part : (k + 1) * part])
+    for k in range(4):
+        term_copy(k).wait_recv()
+        packed[k * n_rows : (k + 1) * n_rows, :] = (oown[k] + orecv[k].astype(F32)).astype(BF16)
+    shape = (4 * n_rows, 4 * n_rows)
+    i, j = iota(shape, 0), iota(shape, 1)
+    spread = onehot(j == (((i & 15) >> 2) * n_rows + (i >> 4) * 4 + (i & 3)))
+    rsend[...] = mm(spread, packed[...]).astype(BF16).reshape(n_exp, 16, part)
+    rrecv[e] = rsend[e]
+
+    def red_copy(d, back=False):
+        to = lax.rem(e + d, n_exp)
+        return remote(
+            rsend.at[to], rrecv.at[to if back else e], r_ss.at[to], r_rs.at[to if back else e], exp=to
+        )
+
+    each(1, n_exp, lambda d: red_copy(d).start())
+    wide = stream[...].astype(F32)
+    base = jnp.concatenate([wide[:, k * part : (k + 1) * part] for k in range(4)], axis=0)
+    each(1, n_exp, lambda d: red_copy(d, True).wait_recv())
+    hidden = (base + jnp.sum(rrecv[...].astype(F32), axis=0)).astype(BF16)
+    blocks[g] = hidden
+
+    def pass_on(number, sem, row=None, exp=None):
+        return remote(blocks.at[number], blocks.at[number], g_ss.at[sem], g_rs.at[number], row=row, exp=exp)
+
+    def arrive(number):
+        remote(blocks.at[number], blocks.at[number], g_ss.at[15], g_rs.at[number], row=1 - r).wait_recv()
+
+    nz = n_exp // 2
+    e_y = z * 2 + (1 - y)
+
+    def own_z(d):
+        pass_on(g, d - 1, exp=lax.rem(z + d, nz) * 2 + y).start()
+
+    pass_on(g, 3, exp=e_y).start()
+    each(1, nz, own_z)
+    pass_on(g, 4, row=1 - r).start()
+
+    def relay_z(d):
+        number = r * n_exp + lax.rem(z + d, nz) * 2 + y
+        arrive(number)
+        pass_on(number, 4 + d, exp=e_y).start()
+        pass_on(number, 7 + d, row=1 - r).start()
+
+    each(1, nz, relay_z)
+
+    def relay_y(d):
+        number = r * n_exp + lax.rem(z + d, nz) * 2 + (1 - y)
+        arrive(number)
+        pass_on(number, 11 + d, row=1 - r).start()
+
+    each(0, nz, relay_y)
+    hw = hidden.astype(F32)
+    for k in range(4):
+        hid4[:, k * part : (k + 1) * part] = hw[4 * k : 4 * k + 4]
+    each(1, devs, lambda d: tile_copy(d, True).wait_recv())
+    slots_n = 2 * devs
+    used = jnp.sum(trecv[...].reshape(devs // 4, 4, 8, 128), axis=1).reshape(slots_n, 128)
+    used = jnp.concatenate([used, used], axis=1)
+    line, col = iota(used.shape, 0), iota(used.shape, 1)
+    used = (used > 0.0) & ((col >> 4) == (line >> 1))
+    each(0, n_exp, lambda j: arrive((1 - r) * n_exp + j))
+
+    sumsq = jnp.zeros((slots_n, 1), F32)
+    flat = blocks[...].reshape(devs * 16, part)
+    for k in range(4):
+        xk = mm(onehot(used & (((col & 15) >> 2) == k)), flat)
+        sumsq += jnp.sum(xk * xk, axis=1, keepdims=True)
+        cut = slice(k * part, (k + 1) * part)
+        xsel[:, cut] = (xk * gain[:, cut]).astype(BF16)
+    sqsend[...] = jnp.broadcast_to(sumsq, sqsend.shape)
+    sq = remote(sqsend, sqrecv, u_ss.at[2], u_rs.at[2], ctx=1 - c)
+    sq.start()
+    weight_copies[3].wait()
+    weight_copies[4].wait()
+    ffe = wg.shape[1]
+    hf = ffe // 2
+
+    def gu_copy(f):
+        return remote(gusend.at[f], gurecv.at[f], u_ss.at[f], u_rs.at[f], ctx=1 - c)
+
+    own = []
+    for f in range(2):
+        cut = slice(f * hf, (f + 1) * hf)
+        gate, up = mm(xsel[...], wg[:, cut]), mm(xsel[...], wu[:, cut])
+        own.append((gate, up))
+        gusend[f, 0:slots_n] = gate.astype(BF16)
+        gusend[f, slots_n : 2 * slots_n] = up.astype(BF16)
+        gu_copy(f).start()
+    sq.wait_recv()
+    inverse = lax.rsqrt((sumsq + sqrecv[:, 0:1]) / D + epsilon)
+    active = []
+    for f in range(2):
+        gu_copy(f).wait_recv()
+        gate = inverse * (own[f][0] + gurecv[f, 0:slots_n].astype(F32))
+        up = inverse * (own[f][1] + gurecv[f, slots_n : 2 * slots_n].astype(F32))
+        active.append((gate / (1.0 + jnp.exp(-gate)) * up).astype(BF16))
+    active = jnp.concatenate(active, axis=1)
+    weight_copies[5].wait()
+    for k in range(7):
+        made[k * slots_n : (k + 1) * slots_n, :] = mm(active, wd[:, k * 512 : (k + 1) * 512]).astype(BF16)
+    shape = (devs * 16, 7 * slots_n)
+    i, j = iota(shape, 0), iota(shape, 1)
+    spread = onehot(j == (((i & 15) >> 1) * slots_n + (i >> 4) * 2 + (i & 1)))
+    psend[...] = mm(spread, made[...]).astype(BF16).reshape(devs, 16, 512)
+    precv[g] = psend[g]
+
+    def back_copy(d, back=False):
+        to = lax.rem(g + d, devs)
+        return remote(
+            psend.at[to], precv.at[to if back else g], p_ss.at[to], p_rs.at[to if back else g],
+            row=to // n_exp, exp=lax.rem(to, n_exp),
+        )
+
+    each(1, devs, lambda d: back_copy(d).start())
+
+    each(1, devs, lambda d: tile_copy(d).wait_send())
+    each(0, rows, lambda b: swap(b).wait_send())
+    for pair in range(2):
+        each(1, n_exp, lambda d: att_copy(pair, d).wait_send())
+    for k in range(4):
+        term_copy(k).wait_send()
+    each(1, n_exp, lambda d: red_copy(d).wait_send())
+    each(0, 15, lambda i: pass_on(g, i, row=1 - r).wait_send())
+    sq.wait_send()
+    for f in range(2):
+        gu_copy(f).wait_send()
+
+    each(1, devs, lambda d: back_copy(d, True).wait_recv())
+    mix = mm(combine[...], precv[...].reshape(devs * 16, 512))
+    mix = mix[0:32] + mix[32:64]
+    for k in range(7):
+        cut = slice(k * 512, (k + 1) * 512)
+        out[:, cut] = (hid4[:, cut] + mix[4 * k : 4 * k + 4]).astype(BF16)
+    each(1, devs, lambda d: back_copy(d).wait_send())
+
+
+def fused(
+    queries, latent_cache, lengths, w_value, w_out, stream, norm_gain, expert_ids, gate_weights,
+    w_gate, w_up, w_down,
+):
+    rows, heads, qk = queries.shape
+    block = latent_cache.shape[1]
+    per_dev, latent, v_head = w_value.shape
+    width = stream.shape[1]
+    n_exp = lax.axis_size("exp")
+    devs = n_exp * lax.axis_size("row")
+    depth, ffe = w_out.shape[0], w_gate.shape[2]
+    part, n_rows, slots_n = width // 4, n_exp * rows, 2 * devs
+    vmem, smem, anyw = (pl.BlockSpec(memory_space=s) for s in (pltpu.VMEM, pltpu.SMEM, pl.ANY))
+    dma = pltpu.SemaphoreType.DMA
+    scratch = [
+        pltpu.VMEM((2, block, qk), BF16),
+        pltpu.VMEM(w_value.shape, BF16),
+        pltpu.VMEM((2, depth, width), BF16),
+        pltpu.VMEM((width, ffe), BF16),
+        pltpu.VMEM((width, ffe), BF16),
+        pltpu.VMEM((ffe, width), BF16),
+        pltpu.VMEM((heads, block), F32),
+        pltpu.VMEM((rows, 2, heads // 2, latent + 128), BF16),
+        pltpu.VMEM((rows, heads // 2, latent + 128), BF16),
+        pltpu.VMEM((n_exp, per_dev, latent), F32),
+        pltpu.VMEM((2, n_exp, 16, latent), BF16),
+        pltpu.VMEM((n_exp, 2, 16, latent), BF16),
+        pltpu.VMEM((n_rows, depth), BF16),
+        pltpu.VMEM((4, n_rows, part), BF16),
+        pltpu.VMEM((4, n_rows, part), F32),
+        pltpu.VMEM((4, n_rows, part), BF16),
+        pltpu.VMEM((4 * n_rows, part), BF16),
+        pltpu.VMEM((n_exp, 16, part), BF16),
+        pltpu.VMEM((n_exp, 16, part), BF16),
+        pltpu.VMEM((rows, width), F32),
+        pltpu.VMEM((devs, 16, part), BF16),
+        pltpu.VMEM((devs, 8, 128), F32),
+        pltpu.VMEM((devs, 8, 128), F32),
+        pltpu.VMEM((slots_n, width), BF16),
+        pltpu.VMEM((2, 2 * slots_n, ffe // 2), BF16),
+        pltpu.VMEM((2, 2 * slots_n, ffe // 2), BF16),
+        pltpu.VMEM((slots_n, 128), F32),
+        pltpu.VMEM((slots_n, 128), F32),
+        pltpu.VMEM((7 * slots_n, 512), BF16),
+        pltpu.VMEM((devs, 16, 512), BF16),
+        pltpu.VMEM((devs, 16, 512), BF16),
+        pltpu.VMEM((64, devs * 16), BF16),
+    ] + [
+        dma(s)
+        for s in (
+            (2,), (6,), (rows,), (rows,), (2, n_exp), (2, n_exp), (4,), (4,), (n_exp,), (n_exp,),
+            (16,), (devs,), (devs,), (devs,), (3,), (3,), (devs,), (devs,),
+        )
+    ]
+    return pl.pallas_call(
+        layer_kernel,
+        out_shape=jax.ShapeDtypeStruct((rows, width), BF16),
+        in_specs=[vmem, anyw, smem, anyw, anyw, vmem, vmem, smem, smem, anyw, anyw, anyw],
+        out_specs=vmem,
+        scratch_shapes=scratch,
+        compiler_params=pltpu.CompilerParams(
+            collective_id=0, has_side_effects=True, vmem_limit_bytes=60 * 1024 * 1024
+        ),
+    )(
+        queries, latent_cache, lengths, w_value, w_out, stream, norm_gain[None, :], expert_ids,
+        gate_weights, w_gate, w_up, w_down,
+    )
+
+
 def solution(mesh):
     placed = (
         P(("row", "exp"), None, None),
@@ -145,6 +608,8 @@
         P(("row", "exp"), "ctx", None),
         P(("row", "exp"), None, "ctx"),
     )
+    sizes = tuple(mesh.shape[axis] for axis in ("ctx", "row", "exp"))
+    body = fused if sizes == (2, 2, 8) else on_device
     return jax.shard_map(
-        on_device, mesh=mesh, in_specs=placed, out_specs=P(("row", "exp"), "ctx"), check_vma=False
-    )
+        body, mesh=mesh, in_specs=placed, out_specs=P(("row", "exp"), "ctx"), check_vma=False
+    )

time: 278 us -> 97.8 us (0.35)
  waiting for transfers between devices: 164 us -> 0 us
  Pallas kernels: 0 us -> 66.4 us
  matrix products: 44 us -> 0 us
  starting transfers between devices: 24.4 us -> 0 us
  local copies, waits for them, and re-layouts: 7.9 us -> 30.5 us
  blocking collectives: 18.8 us -> 0 us
  between operations: 14.3 us -> 0.01 us
  other arithmetic: 4.6 us -> 0 us
    unnamed x3 -> x0, waiting for transfers between devices: 108 us -> none
    pallas_call x0 -> x1, Pallas kernels: none -> 66.4 us  [fused(): pl.pallas_call(layer_kernel, out_shape=jax.ShapeDtypeStruct((rows, width)...]
    dot_general x9 -> x0, matrix products: 44 us -> none  [the longest x1 11.2 us: on_device(): jnp.einsum('bht,btl->bhl', weights.astype(jnp.bfloat16), latent_cache[:,...]
    all_to_all x4 -> x0, waiting for transfers between devices: 40.6 us -> none  [the longest x1 24.3 us: on_device(): lax.all_to_all(latent_out.reshape(1, groups, n_ctx * n_exp, per_dev, late...]
    unnamed x15 -> x3, local copies, waits for them, and re-layouts: 3.82 us -> 29.2 us
    all_to_all x4 -> x0, starting transfers between devices: 24.3 us -> none  [the longest x1 8.31 us: on_device(): lax.all_to_all(totals.reshape(1, groups, n_ctx * n_exp, per_dev), ('ctx',...]
    psum x1 -> x0, waiting for transfers between devices: 15.5 us -> none  [on_device(): gate_part, up_part, sumsq = lax.psum((gate_part, up_part, sumsq), 'ctx')]
    all_to_all x1 -> x0, blocking collectives: 13.8 us -> none  [on_device(): lax.all_to_all(outgoing, ('row', 'exp'), split_axis=0, concat_axis=0, til...]
  transfers between devices with their start and end apart: 6 -> 0, of which waited for: 5 -> 0; matrix products, arithmetic and copies ran while one was open for 5% -> 0% of each run, Pallas kernels for 0% -> 0%
where the time goes in v1:
time: 97.8 us; the launch traced here: 96.9 us
  Pallas kernels  66.4 us (68%)
  local copies, waits for them, and re-layouts  30.5 us (31%)
    pallas_call x1, Pallas kernels, fused(): pl.pallas_call(layer_kernel, out_shape=jax.ShapeDtypeStruct((rows, width)...  66.4 us
    unnamed x3, local copies, waits for them, and re-layouts  29.2 us

profile of v1, /device:TPU:0, one launch (start us, length us, event | category | flops | bytes accessed | tf_op | source)
XLA Modules:
  0.0 96.9 jit_solution(2753953393734098700)
XLA Ops:
  0.0 1.3 %broadcast_in_dim.3.gain = f32[1,3584]{1,0:T(1,128)} reshape(f32[3584]{0:T(1024)} %param.18) | data formatting | bytes 28672 | tf_op jit(solution)/shard_map/broadcast_in_dim | solution.py:591
  1.3 2.1 %copy.13.queries = bf16[4,128,576]{2,1,0:T(8,128)(2,1)} copy(bf16[4,128,576]{1,2,0:T(8,128)(2,1)} %param.12) | data formatting | bytes 1179648 | tf_op args[0]
  3.5 25.6 %copy.14.cache_hbm = bf16[4,4096,576]{2,1,0:T(8,128)(2,1)} copy(bf16[4,4096,576]{1,2,0:T(8,128)(2,1)} %param.13) | data formatting | bytes 37748736 | tf_op args[1]
  29.1 66.4 %shard_map.118 = bf16[4,3584]{1,0:T(4,128)(2,1)} custom-call(bf16[4,128,576]{2,1,0:T(8,128)(2,1)} %copy.13.queries, bf16[4,4096,576]{2,1,0:T(8,128)(2,1)} %copy.14.cache_hbm, s32[4]{0:T(128)} %lengths.1, bf16[8,512,128]{2,1,0:T(8,128)(2,1)} %wv_hbm.1, bf16[1024,7168]{1,0:T(8,128)(2,1)} %wo_hbm.1, bf16[4,3584]{1,0:T(4,128)(2,1)} %stream.1, ...), custom_call_target="tpu_custom_call" | custom-call | tf_op jit(solution)/shard_map/pallas_call | solution.py:581
  95.6 1.4 %copy.16 = bf16[4,3584]{1,0:T(4,128)(2,1)} copy(bf16[4,3584]{1,0:T(4,128)(2,1)} %shard_map.118) | data formatting | bytes 57344

commit v2 on v1

--- a/solution.py
+++ b/solution.py
@@ -171,20 +171,21 @@
     queries, cache_hbm, lengths, wv_hbm, wo_hbm, stream, gain, ids, gates, wg_hbm, wu_hbm, wd_hbm,
     out,
     cache, wv, wo, wg, wu, wd,
-    scores, msg, xr, atf, ats, ar, vals, osend, oown, orecv, packed, rsend, rrecv, hid4, blocks,
+    scores, msg, xr, ats, ar, vals, osend0, oown0, orecv0, rsend0, rrecv0, osend1, oown1, orecv1, rsend1, rrecv1, hid4, blocks,
     tsend, trecv, xsel, gusend, gurecv, sqsend, sqrecv, made, psend, precv, combine,
     cache_sem, w_sem, x_ss, x_rs, a_ss, a_rs, o_ss, o_rs, r_ss, r_rs, g_ss, g_rs, t_ss, t_rs,
     u_ss, u_rs, p_ss, p_rs,
 ):
-    rows, heads, _ = queries.shape
-    block = cache_hbm.shape[1]
+    rows, _, heads = queries.shape
+    block = cache_hbm.shape[2]
     latent = wv_hbm.shape[1]
     n_exp = lax.axis_size("exp")
     devs = lax.axis_size("row") * n_exp
     picks = ids.shape[1]
     per_dev = wv_hbm.shape[0]
     width = stream.shape[1]
-    part = width // 4
+    part, w0 = width // 4, 512
+    w1 = part - w0
     c, r, e = lax.axis_index("ctx"), lax.axis_index("row"), lax.axis_index("exp")
     g = r * n_exp + e
     z, y = e // 2, lax.rem(e, 2)
@@ -241,27 +242,6 @@
 
     each(1, devs, greet)
 
-    shape = (devs, 8, 128)
-    expert, sub, lane = iota(shape, 0), iota(shape, 1), iota(shape, 2)
-    weights, slots = routing(expert, ids, gates, rows, picks)
-    tile = jnp.zeros(shape, F32)
-    for b in range(rows):
-        here = ((lane & 3) == b) & (sub == 2 * lax.rem(g, 4) + slots[b])
-        tile = jnp.where(here, weights[b], tile)
-    tsend[...] = tile
-    trecv[g] = tsend[g]
-
-    shape = (32, devs * 16)
-    line, col = iota(shape, 0), iota(shape, 1)
-    weights, slots = routing(col >> 4, ids, gates, rows, picks)
-    comb = jnp.zeros(shape, F32)
-    for b in range(rows):
-        here = ((line & 3) == b) & ((line >> 2) == ((col & 15) >> 1)) & ((col & 1) == slots[b])
-        comb = jnp.where(here, weights[b], comb)
-    high = comb.astype(BF16)
-    combine[0:32, :] = high
-    combine[32:64, :] = (comb - high.astype(F32)).astype(BF16)
-
     pl.semaphore_wait(barrier, devs)
 
     def tile_copy(d, back=False):
@@ -271,30 +251,26 @@
             row=to // n_exp, exp=lax.rem(to, n_exp),
         )
 
-    each(1, devs, lambda d: tile_copy(d).start())
-
     def swap(b):
         return remote(msg.at[b, 1 - c], xr.at[b], x_ss.at[b], x_rs.at[b], ctx=1 - c)
 
-    def att_copy(pair, d, back=False):
+    def att_copy(b, d, back=False):
         to = lax.rem(e + d, n_exp)
         return remote(
-            ats.at[pair, to], ar.at[to if back else e, pair],
-            a_ss.at[pair, to], a_rs.at[pair, to if back else e], exp=to,
+            ats.at[b, to], ar.at[to if back else e, b],
+            a_ss.at[b, to], a_rs.at[b, to if back else e], exp=to,
         )
 
     def attend(b):
         slot = lax.rem(b, 2)
         cache_copy(b).wait()
-        query = queries[b]
+        query = queries[b].T
         live = lengths[b] - c * block
         step = 1024
         tops = []
         for t in range(block // step):
             span = slice(t * step, (t + 1) * step)
-            s = lax.dot_general(
-                query, cache[slot, span, :], (((1,), (1,)), ((), ())), preferred_element_type=F32
-            )
+            s = mm(query, cache[slot, :, span])
             s = jnp.where(iota(s.shape, 1) + t * step < live, s, DEAD)
             scores[:, span] = s
             tops.append(jnp.max(s, axis=1, keepdims=True))
@@ -308,7 +284,10 @@
             span = slice(t * step, (t + 1) * step)
             p = jnp.exp2((scores[:, span] - top) * RATE)
             total += jnp.sum(p, axis=1, keepdims=True)
-            acc += mm(p.astype(BF16), cache[slot, span, 0:latent])
+            acc += lax.dot_general(
+                p.astype(BF16), cache[slot, 0:latent, span], (((1,), (1,)), ((), ())),
+                preferred_element_type=F32,
+            )
         lane = iota((heads, 128), 1)
         rest = total - total.astype(BF16).astype(F32)
         aux = jnp.where(lane == 0, top, jnp.where(lane == 1, total, jnp.where(lane == 2, rest, 0.0)))
@@ -319,7 +298,7 @@
             msg[b, side, :, latent : latent + 128] = aux[mine]
         swap(b).start()
 
-    def merge(b, pair, last):
+    def merge(b):
         swap(b).wait_recv()
         one, two = msg[b, c].astype(F32), xr[b].astype(F32)
 
@@ -332,12 +311,10 @@
         inv = 1.0 / (f1 * sum1 + f2 * sum2)
         att = (f1 * inv) * one[:, 0:latent] + (f2 * inv) * two[:, 0:latent]
         att = att.reshape(n_exp, per_dev, latent)
-        if not last:
-            atf[...] = att
-        else:
-            ats[pair] = jnp.concatenate([atf[...], att], axis=1).astype(BF16)
-            ar[e, pair] = ats[pair, e]
-            each(1, n_exp, lambda d: att_copy(pair, d).start())
+        half = latent // 2
+        ats[b] = jnp.concatenate([att[:, :, 0:half], att[:, :, half:]], axis=1).astype(BF16)
+        ar[e, b] = ats[b, e]
+        each(1, n_exp, lambda d: att_copy(b, d).start())
 
     def row_step(b):
         attend(b)
@@ -348,65 +325,89 @@
 
         @pl.when(b == 1)
         def _():
-            merge(0, 0, False)
+            merge(0)
             for w in weight_copies[0:3]:
                 w.start()
 
         @pl.when(b == 2)
         def _():
-            merge(1, 0, True)
+            merge(1)
             for w in weight_copies[3:5]:
                 w.start()
 
         @pl.when(b == 3)
         def _():
-            merge(2, 1, False)
+            merge(2)
             weight_copies[5].start()
 
     each(0, rows, row_step)
-    merge(3, 1, True)
+    merge(3)
+
+    shape = (devs, 8, 128)
+    expert, sub, lane = iota(shape, 0), iota(shape, 1), iota(shape, 2)
+    weights, slots = routing(expert, ids, gates, rows, picks)
+    tile = jnp.zeros(shape, F32)
+    for b in range(rows):
+        here = ((lane & 3) == b) & (sub == 2 * lax.rem(g, 4) + slots[b])
+        tile = jnp.where(here, weights[b], tile)
+    tsend[...] = tile
+    trecv[g] = tsend[g]
+    each(1, devs, lambda d: tile_copy(d).start())
 
     weight_copies[0].wait()
-    for pair in range(2):
-        each(1, n_exp, lambda d: att_copy(pair, d, True).wait_recv())
+    for b in range(rows):
+        each(1, n_exp, lambda d: att_copy(b, d, True).wait_recv())
     n_rows = n_exp * rows
-    x = ar[...].reshape(n_rows * per_dev, latent)
+    x = ar[...].astype(F32).reshape(n_rows, 2, per_dev, latent // 2)
+    x = jnp.concatenate([x[:, 0], x[:, 1]], axis=2).reshape(n_rows * per_dev, latent).astype(BF16)
     for h in range(per_dev):
         v = mm(x, wv[h])
         v = jnp.where((iota(v.shape, 0) & (per_dev - 1)) == h, v, 0.0)
         v = jnp.sum(v.reshape(n_rows, per_dev, v.shape[1]), axis=1)
         vals[:, h * v.shape[1] : (h + 1) * v.shape[1]] = v.astype(BF16)
 
-    def term_copy(k):
-        return remote(osend.at[k], orecv.at[k], o_ss.at[k], o_rs.at[k], ctx=1 - c)
+    def cuts(k):
+        return slice(k * w0, (k + 1) * w0), slice(4 * w0 + k * w1, 4 * w0 + (k + 1) * w1)
+
+    osend, oown, orecv, rsend, rrecv = (osend0, osend1), (oown0, oown1), (orecv0, orecv1), (rsend0, rsend1), (rrecv0, rrecv1)
+
+    def term_copy(q):
+        return remote(osend[q], orecv[q], o_ss.at[q], o_rs.at[q], ctx=1 - c)
+
+    def red_copy(q, d, back=False):
+        to = lax.rem(e + d, n_exp)
+        return remote(
+            rsend[q].at[to], rrecv[q].at[to if back else e],
+            r_ss.at[q, to], r_rs.at[q, to if back else e], exp=to,
+        )
 
     weight_copies[1].wait()
-    for k in range(4):
-        osend[k] = mm(vals[...], wo[0, :, k * part : (k + 1) * part]).astype(BF16)
-        term_copy(k).start()
+    for q in range(2):
+        for k in range(4):
+            osend[q][k] = mm(vals[...], wo[0, :, cuts(k)[q]]).astype(BF16)
+        term_copy(q).start()
     weight_copies[2].wait()
-    for k in range(4):
-        oown[k] = mm(vals[...], wo[1, :, k * part : (k + 1) * part])
-    for k in range(4):
-        term_copy(k).wait_recv()
-        packed[k * n_rows : (k + 1) * n_rows, :] = (oown[k] + orecv[k].astype(F32)).astype(BF16)
     shape = (4 * n_rows, 4 * n_rows)
     i, j = iota(shape, 0), iota(shape, 1)
     spread = onehot(j == (((i & 15) >> 2) * n_rows + (i >> 4) * 4 + (i & 3)))
-    rsend[...] = mm(spread, packed[...]).astype(BF16).reshape(n_exp, 16, part)
-    rrecv[e] = rsend[e]
-
-    def red_copy(d, back=False):
-        to = lax.rem(e + d, n_exp)
-        return remote(
-            rsend.at[to], rrecv.at[to if back else e], r_ss.at[to], r_rs.at[to if back else e], exp=to
-        )
-
-    each(1, n_exp, lambda d: red_copy(d).start())
+    for q in range(2):
+        for k in range(4):
+            oown[q][k] = mm(vals[...], wo[1, :, cuts(k)[q]])
+    for q in range(2):
+        term_copy(q).wait_recv()
+        both = oown[q][...] + orecv[q][...].astype(F32)
+        both = both.reshape(4 * n_rows, both.shape[2]).astype(BF16)
+        rsend[q][...] = mm(spread, both).astype(BF16).reshape(rsend[q].shape)
+        rrecv[q][e] = rsend[q][e]
+        each(1, n_exp, lambda d: red_copy(q, d).start())
     wide = stream[...].astype(F32)
-    base = jnp.concatenate([wide[:, k * part : (k + 1) * part] for k in range(4)], axis=0)
-    each(1, n_exp, lambda d: red_copy(d, True).wait_recv())
-    hidden = (base + jnp.sum(rrecv[...].astype(F32), axis=0)).astype(BF16)
+    base = jnp.concatenate(
+        [jnp.concatenate([wide[:, cut] for cut in cuts(k)], axis=1) for k in range(4)], axis=0
+    )
+    for q in range(2):
+        each(1, n_exp, lambda d: red_copy(q, d, True).wait_recv())
+    attn = jnp.concatenate([jnp.sum(rrecv[q][...].astype(F32), axis=0) for q in range(2)], axis=1)
+    hidden = (base + attn).astype(BF16)
     blocks[g] = hidden
 
     def pass_on(number, sem, row=None, exp=None):
@@ -441,7 +442,8 @@
     each(0, nz, relay_y)
     hw = hidden.astype(F32)
     for k in range(4):
-        hid4[:, k * part : (k + 1) * part] = hw[4 * k : 4 * k + 4]
+        for cut, lanes in zip(cuts(k), (slice(0, w0), slice(w0, part))):
+            hid4[:, cut] = hw[4 * k : 4 * k + 4, lanes]
     each(1, devs, lambda d: tile_copy(d, True).wait_recv())
     slots_n = 2 * devs
     used = jnp.sum(trecv[...].reshape(devs // 4, 4, 8, 128), axis=1).reshape(slots_n, 128)
@@ -451,12 +453,13 @@
     each(0, n_exp, lambda j: arrive((1 - r) * n_exp + j))
 
     sumsq = jnp.zeros((slots_n, 1), F32)
+    scale = gain[...].reshape(1, width)
     flat = blocks[...].reshape(devs * 16, part)
     for k in range(4):
         xk = mm(onehot(used & (((col & 15) >> 2) == k)), flat)
         sumsq += jnp.sum(xk * xk, axis=1, keepdims=True)
-        cut = slice(k * part, (k + 1) * part)
-        xsel[:, cut] = (xk * gain[:, cut]).astype(BF16)
+        for cut, lanes in zip(cuts(k), (slice(0, w0), slice(w0, part))):
+            xsel[:, cut] = (xk[:, lanes] * scale[:, cut]).astype(BF16)
     sqsend[...] = jnp.broadcast_to(sumsq, sqsend.shape)
     sq = remote(sqsend, sqrecv, u_ss.at[2], u_rs.at[2], ctx=1 - c)
     sq.start()
@@ -503,13 +506,24 @@
 
     each(1, devs, lambda d: back_copy(d).start())
 
+    shape = (32, devs * 16)
+    line, col = iota(shape, 0), iota(shape, 1)
+    weights, slots = routing(col >> 4, ids, gates, rows, picks)
+    comb = jnp.zeros(shape, F32)
+    for b in range(rows):
+        here = ((line & 3) == b) & ((line >> 2) == ((col & 15) >> 1)) & ((col & 1) == slots[b])
+        comb = jnp.where(here, weights[b], comb)
+    high = comb.astype(BF16)
+    combine[0:32, :] = high
+    combine[32:64, :] = (comb - high.astype(F32)).astype(BF16)
+
     each(1, devs, lambda d: tile_copy(d).wait_send())
     each(0, rows, lambda b: swap(b).wait_send())
-    for pair in range(2):
-        each(1, n_exp, lambda d: att_copy(pair, d).wait_send())
-    for k in range(4):
-        term_copy(k).wait_send()
-    each(1, n_exp, lambda d: red_copy(d).wait_send())
+    for b in range(rows):
+        each(1, n_exp, lambda d: att_copy(b, d).wait_send())
+    for q in range(2):
+        term_copy(q).wait_send()
+        each(1, n_exp, lambda d: red_copy(q, d).wait_send())
     each(0, 15, lambda i: pass_on(g, i, row=1 - r).wait_send())
     sq.wait_send()
     for f in range(2):
@@ -539,7 +553,7 @@
     vmem, smem, anyw = (pl.BlockSpec(memory_space=s) for s in (pltpu.VMEM, pltpu.SMEM, pl.ANY))
     dma = pltpu.SemaphoreType.DMA
     scratch = [
-        pltpu.VMEM((2, block, qk), BF16),
+        pltpu.VMEM((2, qk, block), BF16),
         pltpu.VMEM(w_value.shape, BF16),
         pltpu.VMEM((2, depth, width), BF16),
         pltpu.VMEM((width, ffe), BF16),
@@ -548,16 +562,20 @@
         pltpu.VMEM((heads, block), F32),
         pltpu.VMEM((rows, 2, heads // 2, latent + 128), BF16),
         pltpu.VMEM((rows, heads // 2, latent + 128), BF16),
-        pltpu.VMEM((n_exp, per_dev, latent), F32),
-        pltpu.VMEM((2, n_exp, 16, latent), BF16),
-        pltpu.VMEM((n_exp, 2, 16, latent), BF16),
+        pltpu.VMEM((rows, n_exp, 16, latent // 2), BF16),
+        pltpu.VMEM((n_exp, rows, 16, latent // 2), BF16),
         pltpu.VMEM((n_rows, depth), BF16),
-        pltpu.VMEM((4, n_rows, part), BF16),
-        pltpu.VMEM((4, n_rows, part), F32),
-        pltpu.VMEM((4, n_rows, part), BF16),
-        pltpu.VMEM((4 * n_rows, part), BF16),
-        pltpu.VMEM((n_exp, 16, part), BF16),
-        pltpu.VMEM((n_exp, 16, part), BF16),
+        *(
+            buffer
+            for piece in (512, part - 512)
+            for buffer in (
+                pltpu.VMEM((4, n_rows, piece), BF16),
+                pltpu.VMEM((4, n_rows, piece), F32),
+                pltpu.VMEM((4, n_rows, piece), BF16),
+                pltpu.VMEM((n_exp, 16, piece), BF16),
+                pltpu.VMEM((n_exp, 16, piece), BF16),
+            )
+        ),
         pltpu.VMEM((rows, width), F32),
         pltpu.VMEM((devs, 16, part), BF16),
         pltpu.VMEM((devs, 8, 128), F32),
@@ -574,7 +592,7 @@
     ] + [
         dma(s)
         for s in (
-            (2,), (6,), (rows,), (rows,), (2, n_exp), (2, n_exp), (4,), (4,), (n_exp,), (n_exp,),
+            (2,), (6,), (rows,), (rows,), (rows, n_exp), (rows, n_exp), (2,), (2,), (2, n_exp), (2, n_exp),
             (16,), (devs,), (devs,), (devs,), (3,), (3,), (devs,), (devs,),
         )
     ]
@@ -588,8 +606,8 @@
             collective_id=0, has_side_effects=True, vmem_limit_bytes=60 * 1024 * 1024
         ),
     )(
-        queries, latent_cache, lengths, w_value, w_out, stream, norm_gain[None, :], expert_ids,
-        gate_weights, w_gate, w_up, w_down,
+        jnp.swapaxes(queries, 1, 2), jnp.swapaxes(latent_cache, 1, 2), lengths, w_value, w_out, stream,
+        norm_gain, expert_ids, gate_weights, w_gate, w_up, w_down,
     )
 
 

time: 97.8 us -> 67.9 us (0.69)
  local copies, waits for them, and re-layouts: 30.5 us -> 1.37 us
    unnamed x3 -> x1, local copies, waits for them, and re-layouts: 29.2 us -> 1.37 us
    broadcast_in_dim x1 -> x0, local copies, waits for them, and re-layouts: 1.33 us -> none  [fused(): norm_gain[None, :]]
where the time goes in v2:
time: 67.9 us; the launch traced here: 67.7 us
  Pallas kernels  66.4 us (98%)
  local copies, waits for them, and re-layouts  1.37 us (2%)
    pallas_call x1, Pallas kernels, fused(): pl.pallas_call(layer_kernel, out_shape=jax.ShapeDtypeStruct((rows, width)...  66.4 us
    unnamed x1, local copies, waits for them, and re-layouts  1.37 us

profile of v2, /device:TPU:0, one launch (start us, length us, event | category | flops | bytes accessed | tf_op | source)
XLA Modules:
  0.0 67.7 jit_solution(1919805926747322510)
XLA Ops:
  0.0 66.4 %shard_map.118 = bf16[4,3584]{1,0:T(4,128)(2,1)} custom-call(bf16[4,576,128]{2,1,0:T(8,128)(2,1)} %bitcast.3, bf16[4,576,4096]{2,1,0:T(8,128)(2,1)} %bitcast.2, s32[4]{0:T(128)} %lengths.1, bf16[8,512,128]{2,1,0:T(8,128)(2,1)} %wv_hbm.1, bf16[1024,7168]{1,0:T(8,128)(2,1)} %wo_hbm.1, bf16[4,3584]{1,0:T(4,128)(2,1)} %stream.1, f32[3584]{0:T(1024)} %gain.1, ...), custom_call_target="tpu_custom_call" | custom-call | tf_op jit(solution)/shard_map/pallas_call | solution.py:599
  66.4 1.4 %copy.14 = bf16[4,3584]{1,0:T(4,128)(2,1)} copy(bf16[4,3584]{1,0:T(4,128)(2,1)} %shard_map.118) | data formatting | bytes 57344

commit v3 on v2

--- a/solution.py
+++ b/solution.py
@@ -201,12 +201,12 @@
             src_ref=src, dst_ref=dst, send_sem=ss, recv_sem=rs, device_id=where, device_id_type=MESH
         )
 
-    def each(low, high, body):
+    def each(low, high, body, unroll=True):
         def step(i, carry):
             body(i)
             return carry
 
-        lax.fori_loop(low, high, step, 0)
+        lax.fori_loop(low, high, step, 0, unroll=unroll)
 
     def cache_copy(b):
         slot = lax.rem(b, 2)
@@ -279,19 +279,19 @@
             top = jnp.maximum(top, other)
         top = jnp.maximum(top, FLOOR).astype(BF16).astype(F32)
         total = jnp.zeros_like(top)
-        acc = jnp.zeros((heads, latent), F32)
+        acc = jnp.zeros((latent, heads), F32)
         for t in range(block // step):
             span = slice(t * step, (t + 1) * step)
             p = jnp.exp2((scores[:, span] - top) * RATE)
             total += jnp.sum(p, axis=1, keepdims=True)
             acc += lax.dot_general(
-                p.astype(BF16), cache[slot, 0:latent, span], (((1,), (1,)), ((), ())),
+                cache[slot, 0:latent, span], p.astype(BF16), (((1,), (1,)), ((), ())),
                 preferred_element_type=F32,
             )
         lane = iota((heads, 128), 1)
         rest = total - total.astype(BF16).astype(F32)
         aux = jnp.where(lane == 0, top, jnp.where(lane == 1, total, jnp.where(lane == 2, rest, 0.0)))
-        acc, aux = acc.astype(BF16), aux.astype(BF16)
+        acc, aux = acc.T.astype(BF16), aux.astype(BF16)
         for side in range(2):
             mine = slice(side * half_heads, (side + 1) * half_heads)
             msg[b, side, :, 0:latent] = acc[mine]
@@ -340,7 +340,7 @@
             merge(2)
             weight_copies[5].start()
 
-    each(0, rows, row_step)
+    each(0, rows, row_step, False)
     merge(3)
 
     shape = (devs, 8, 128)
@@ -393,7 +393,6 @@
     for q in range(2):
         for k in range(4):
             oown[q][k] = mm(vals[...], wo[1, :, cuts(k)[q]])
-    for q in range(2):
         term_copy(q).wait_recv()
         both = oown[q][...] + orecv[q][...].astype(F32)
         both = both.reshape(4 * n_rows, both.shape[2]).astype(BF16)

time: 67.9 us -> 67.2 us (0.990)
  Pallas kernels: 66.4 us -> 65.6 us
    pallas_call x1, Pallas kernels: 66.4 us -> 65.6 us  [fused(): pl.pallas_call(layer_kernel, out_shape=jax.ShapeDtypeStruct((rows, width)...]
where the time goes in v3:
time: 67.2 us; the launch traced here: 67 us
  Pallas kernels  65.6 us (98%)
  local copies, waits for them, and re-layouts  1.37 us (2%)
    pallas_call x1, Pallas kernels, fused(): pl.pallas_call(layer_kernel, out_shape=jax.ShapeDtypeStruct((rows, width)...  65.6 us
    unnamed x1, local copies, waits for them, and re-layouts  1.37 us

profile of v3, /device:TPU:0, one launch (start us, length us, event | category | flops | bytes accessed | tf_op | source)
XLA Modules:
  0.0 67.0 jit_solution(14321684894147863748)
XLA Ops:
  0.0 65.6 %shard_map.118 = bf16[4,3584]{1,0:T(4,128)(2,1)} custom-call(bf16[4,576,128]{2,1,0:T(8,128)(2,1)} %bitcast.3, bf16[4,576,4096]{2,1,0:T(8,128)(2,1)} %bitcast.2, s32[4]{0:T(128)} %lengths.1, bf16[8,512,128]{2,1,0:T(8,128)(2,1)} %wv_hbm.1, bf16[1024,7168]{1,0:T(8,128)(2,1)} %wo_hbm.1, bf16[4,3584]{1,0:T(4,128)(2,1)} %stream.1, f32[3584]{0:T(1024)} %gain.1, ...), custom_call_target="tpu_custom_call" | custom-call | tf_op jit(solution)/shard_map/pallas_call | solution.py:598
  65.6 1.4 %copy.14 = bf16[4,3584]{1,0:T(4,128)(2,1)} copy(bf16[4,3584]{1,0:T(4,128)(2,1)} %shard_map.118) | data formatting | bytes 57344

commit v4 on v3

--- a/solution.py
+++ b/solution.py
@@ -208,21 +208,54 @@
 
         lax.fori_loop(low, high, step, 0, unroll=unroll)
 
+    class Pieces:
+        def __init__(self, copies):
+            self.copies = copies
+
+        def start(self):
+            for copy in self.copies:
+                copy.start()
+
+        def wait(self):
+            for copy in self.copies:
+                copy.wait()
+
     def cache_copy(b):
         slot = lax.rem(b, 2)
-        return pltpu.make_async_copy(cache_hbm.at[b], cache.at[slot], cache_sem.at[slot])
+        step = cache_hbm.shape[1] // 4
+        return Pieces(
+            [
+                pltpu.make_async_copy(
+                    cache_hbm.at[b, i * step : (i + 1) * step],
+                    cache.at[slot, i * step : (i + 1) * step],
+                    cache_sem.at[slot, i],
+                )
+                for i in range(4)
+            ]
+        )
+
+    def in_pieces(src, dst, number):
+        step = dst.shape[0] // 4
+        return Pieces(
+            [
+                pltpu.make_async_copy(
+                    src.at[i * step : (i + 1) * step], dst.at[i * step : (i + 1) * step], w_sem.at[number, i]
+                )
+                for i in range(4)
+            ]
+        )
 
     def half_of(i):
         side = (1 - c) if i == 0 else c
         return wo_hbm.at[:, pl.ds(pl.multiple_of(side * width, 128), width)]
 
     weight_copies = [
-        pltpu.make_async_copy(wv_hbm, wv, w_sem.at[0]),
-        pltpu.make_async_copy(half_of(0), wo.at[0], w_sem.at[1]),
-        pltpu.make_async_copy(half_of(1), wo.at[1], w_sem.at[2]),
-        pltpu.make_async_copy(wg_hbm.at[0], wg, w_sem.at[3]),
-        pltpu.make_async_copy(wu_hbm.at[0], wu, w_sem.at[4]),
-        pltpu.make_async_copy(wd_hbm.at[0], wd, w_sem.at[5]),
+        in_pieces(wv_hbm, wv, 0),
+        in_pieces(half_of(0), wo.at[0], 1),
+        in_pieces(half_of(1), wo.at[1], 2),
+        in_pieces(wg_hbm.at[0], wg, 3),
+        in_pieces(wu_hbm.at[0], wu, 4),
+        in_pieces(wd_hbm.at[0], wd, 5),
     ]
 
     cache_copy(0).start()
@@ -488,22 +521,27 @@
         active.append((gate / (1.0 + jnp.exp(-gate)) * up).astype(BF16))
     active = jnp.concatenate(active, axis=1)
     weight_copies[5].wait()
-    for k in range(7):
-        made[k * slots_n : (k + 1) * slots_n, :] = mm(active, wd[:, k * 512 : (k + 1) * 512]).astype(BF16)
-    shape = (devs * 16, 7 * slots_n)
+    shape = (devs * 16, 8 * slots_n)
     i, j = iota(shape, 0), iota(shape, 1)
     spread = onehot(j == (((i & 15) >> 1) * slots_n + (i >> 4) * 2 + (i & 1)))
-    psend[...] = mm(spread, made[...]).astype(BF16).reshape(devs, 16, 512)
-    precv[g] = psend[g]
-
-    def back_copy(d, back=False):
+
+    def back_copy(q, d, back=False):
         to = lax.rem(g + d, devs)
         return remote(
-            psend.at[to], precv.at[to if back else g], p_ss.at[to], p_rs.at[to if back else g],
+            psend.at[q, to], precv.at[q, to if back else g], p_ss.at[q, to], p_rs.at[q, to if back else g],
             row=to // n_exp, exp=lax.rem(to, n_exp),
         )
 
-    each(1, devs, lambda d: back_copy(d).start())
+    parts = ((0, 8), (8, width // 256))
+    for q, (low, high) in enumerate(parts):
+        for k in range(low, high):
+            row = (k - low) * slots_n
+            made[row : row + slots_n, :] = mm(active, wd[:, k * 256 : (k + 1) * 256]).astype(BF16)
+        used_rows = (high - low) * slots_n
+        sent = mm(spread[:, 0:used_rows], made[0:used_rows, :])
+        psend[q] = sent.astype(BF16).reshape(devs, 16, 256)
+        precv[q, g] = psend[q, g]
+        each(1, devs, lambda d: back_copy(q, d).start())
 
     shape = (32, devs * 16)
     line, col = iota(shape, 0), iota(shape, 1)
@@ -528,13 +566,15 @@
     for f in range(2):
         gu_copy(f).wait_send()
 
-    each(1, devs, lambda d: back_copy(d, True).wait_recv())
-    mix = mm(combine[...], precv[...].reshape(devs * 16, 512))
-    mix = mix[0:32] + mix[32:64]
-    for k in range(7):
-        cut = slice(k * 512, (k + 1) * 512)
-        out[:, cut] = (hid4[:, cut] + mix[4 * k : 4 * k + 4]).astype(BF16)
-    each(1, devs, lambda d: back_copy(d).wait_send())
+    for q, (low, high) in enumerate(parts):
+        each(1, devs, lambda d: back_copy(q, d, True).wait_recv())
+        mix = mm(combine[...], precv[q].reshape(devs * 16, 256))
+        mix = mix[0:32] + mix[32:64]
+        for k in range(low, high):
+            cut = slice(k * 256, (k + 1) * 256)
+            out[:, cut] = (hid4[:, cut] + mix[4 * (k - low) : 4 * (k - low) + 4]).astype(BF16)
+    for q in range(2):
+        each(1, devs, lambda d: back_copy(q, d).wait_send())
 
 
 def fused(
@@ -584,15 +624,15 @@
         pltpu.VMEM((2, 2 * slots_n, ffe // 2), BF16),
         pltpu.VMEM((slots_n, 128), F32),
         pltpu.VMEM((slots_n, 128), F32),
-        pltpu.VMEM((7 * slots_n, 512), BF16),
-        pltpu.VMEM((devs, 16, 512), BF16),
-        pltpu.VMEM((devs, 16, 512), BF16),
+        pltpu.VMEM((8 * slots_n, 256), BF16),
+        pltpu.VMEM((2, devs, 16, 256), BF16),
+        pltpu.VMEM((2, devs, 16, 256), BF16),
         pltpu.VMEM((64, devs * 16), BF16),
     ] + [
         dma(s)
         for s in (
-            (2,), (6,), (rows,), (rows,), (rows, n_exp), (rows, n_exp), (2,), (2,), (2, n_exp), (2, n_exp),
-            (16,), (devs,), (devs,), (devs,), (3,), (3,), (devs,), (devs,),
+            (2, 4), (6, 4), (rows,), (rows,), (rows, n_exp), (rows, n_exp), (2,), (2,), (2, n_exp), (2, n_exp),
+            (16,), (devs,), (devs,), (devs,), (3,), (3,), (2, devs), (2, devs),
         )
     ]
     return pl.pallas_call(

time: 67.2 us -> 67.5 us (level)
  no operation moved by 1% of the time
where the time goes in v4:
time: 67.5 us; the launch traced here: 67.3 us
  Pallas kernels  65.9 us (98%)
  local copies, waits for them, and re-layouts  1.37 us (2%)
    pallas_call x1, Pallas kernels, fused(): pl.pallas_call(layer_kernel, out_shape=jax.ShapeDtypeStruct((rows, width)...  65.9 us
    unnamed x1, local copies, waits for them, and re-layouts  1.37 us

profile of v4, /device:TPU:0, one launch (start us, length us, event | category | flops | bytes accessed | tf_op | source)
XLA Modules:
  0.0 67.3 jit_solution(16209813147264537463)
XLA Ops:
  0.0 65.9 %shard_map.118 = bf16[4,3584]{1,0:T(4,128)(2,1)} custom-call(bf16[4,576,128]{2,1,0:T(8,128)(2,1)} %bitcast.3, bf16[4,576,4096]{2,1,0:T(8,128)(2,1)} %bitcast.2, s32[4]{0:T(128)} %lengths.1, bf16[8,512,128]{2,1,0:T(8,128)(2,1)} %wv_hbm.1, bf16[1024,7168]{1,0:T(8,128)(2,1)} %wo_hbm.1, bf16[4,3584]{1,0:T(4,128)(2,1)} %stream.1, f32[3584]{0:T(1024)} %gain.1, ...), custom_call_target="tpu_custom_call" | custom-call | tf_op jit(solution)/shard_map/pallas_call | solution.py:638
  65.9 1.4 %copy.14 = bf16[4,3584]{1,0:T(4,128)(2,1)} copy(bf16[4,3584]{1,0:T(4,128)(2,1)} %shard_map.118) | data formatting | bytes 57344
